TPU v7x, 256 devices: a whole 4x4x8 slice. The times are simulated.
256 devices in a mesh: outer: 16 (over z, y_hi), inner: 16 (over y_lo, x, core).
Axes of the slice: x: 4, y: 4 (y_hi: 2, y_lo: 2; y = y_hi * 2 + y_lo), z: 8, core: 2. Of those that a mesh axis runs over, the one named last changes fastest.
Arguments:
- queries: bfloat16 [32768, 32, 128], P(('outer', 'inner')), may hold values from -6 to 6
- keys: bfloat16 [32768, 4, 128], P(('outer', 'inner')), may hold values from -6 to 6
- values: bfloat16 [32768, 4, 128], P(('outer', 'inner')), may hold values from -6 to 6
- output_gradient: bfloat16 [32768, 32, 128], P(('outer', 'inner')), may hold values from -6 to 6
- kept_offset: int32 [256, 128], replicated, may hold values from 0 to 1024, as said below
- region_pos: int32 [256], replicated, may hold values from 0 to 255, each once
Outputs:
- attn_out: bfloat16 [32768, 32, 128], P(('outer', 'inner'))
- grad_queries: bfloat16 [32768, 32, 128], P(('outer', 'inner'))
- key_gradient: bfloat16 [32768, 4, 128], P(('outer', 'inner'))
- value_gradient: bfloat16 [32768, 4, 128], P(('outer', 'inner'))
Inputs may be any that keep to these rules, and one draw needn't show every extreme that they name: In each row of kept_offset the live slots (values under 1024) come first and strictly increase; the remaining slots hold 1024. Every shard has at least two live slots, some shard has all 128 live with offset 0 in its first slot, and some shard has empty slots.
All inputs are finite; a program needn't handle non-finite values.
Results may differ from a plain program's by a relative error of at most 0.025.
Values may be sent and summed in bfloat16 or wider, within the bound.
No kernel may reach another device: no remote copies, remote signals or barrier semaphores. Data moves between devices by JAX's collectives and lax.ppermute only.
A program may use at most 128 MiB of HBM per device.

v0:
```python
import jax
import jax.numpy as jnp
from jax import lax
from jax.sharding import PartitionSpec as P

REGION = 1024


masked_fill = -1e30


def passed_along(block, axis, distance):
    devices = range(lax.axis_size(axis))
    route = [((i - distance) % len(devices), i) for i in devices]
    return lax.ppermute(block, axis, route)


def as_sent(shard):

    def short(part):
        return part.astype(jnp.bfloat16) if part.dtype == jnp.float32 else part

    return jax.tree.map(short, shard)


def on_device(queries, keys, values, output_gradient, kept_offset, region_pos):
    slots, heads_q, width = queries.shape
    heads_kv = keys.shape[1]
    context_group = heads_q // heads_kv
    scale = width ** (-0.5)
    inner_count = lax.axis_size("inner")
    outer_count = lax.axis_size("outer")
    outer_id = lax.axis_index("outer")
    inner_id = lax.axis_index("inner")
    device = outer_id * inner_count + inner_id
    live_all = kept_offset < REGION
    live_rows = lax.dynamic_index_in_dim(live_all, device, 0, keepdims=False)
    my_place = lax.dynamic_index_in_dim(region_pos, device, 0, keepdims=False)
    q_four = queries.reshape(slots, heads_kv, context_group, width)
    grad_four = output_gradient.reshape(slots, heads_kv, context_group, width)
    positions = jnp.arange(slots)
    causal = positions[None, :] <= positions[:, None]

    def tile_mask(group_id, block):
        source = group_id * inner_count + block
        key_live = lax.dynamic_index_in_dim(live_all, source, 0, keepdims=False)
        place = lax.dynamic_index_in_dim(region_pos, source, 0, keepdims=False)
        earlier = place < my_place
        same = source == device
        mask = live_rows[:, None] & key_live[None, :] & (earlier | same & causal)
        return (mask, earlier | same)

    def collect_group(both):
        return (
            lax.all_gather(both[0], "inner", axis=0, tiled=True),
            lax.all_gather(both[1], "inner", axis=0, tiled=True),
        )

    own_group = collect_group((keys, values))
    prev_pair = passed_along((keys, values), "outer", 1)
    prev_group = collect_group(prev_pair)
    rounds = ((own_group, outer_id), (prev_group, (outer_id - 1) % outer_count))

    def block_pair(both, block):
        key_block = lax.dynamic_slice_in_dim(both[0], block * slots, slots, 0)
        value_block = lax.dynamic_slice_in_dim(both[1], block * slots, slots, 0)
        return (key_block, value_block)

    def scores_of(key_block):
        return (
            jnp.einsum("tgjc,ugc->gjtu", q_four, key_block, preferred_element_type=jnp.float32)
            * scale
        )

    state = (
        jnp.full((heads_kv, context_group, slots), masked_fill, jnp.float32),
        jnp.zeros((heads_kv, context_group, slots), jnp.float32),
        jnp.zeros((heads_kv, context_group, slots, width), jnp.float32),
    )
    for both, group_id in rounds:

        def forward_step(block, carry, both=both, group_id=group_id):
            mask, needed = tile_mask(group_id, block)
            key_block, value_block = block_pair(both, block)

            def forward_work(inner_carry):
                run_max, run_total, run_acc = inner_carry
                scores = scores_of(key_block)
                new_max = jnp.maximum(
                    run_max, jnp.max(jnp.where(mask, scores, masked_fill), axis=-1)
                )
                factor = jnp.exp(run_max - new_max)
                weights = jnp.where(mask, jnp.exp(scores - new_max[..., None]), 0.0)
                new_total = run_total * factor + jnp.sum(weights, axis=-1)
                update = jnp.einsum(
                    "gjtu,ugc->gjtc",
                    weights.astype(jnp.bfloat16),
                    value_block,
                    preferred_element_type=jnp.float32,
                )
                return (new_max, new_total, run_acc * factor[..., None] + update)

            return lax.cond(needed, forward_work, lambda inner_carry: inner_carry, carry)

        state = lax.fori_loop(0, inner_count, forward_step, state)
    row_max, total, accum = state
    safe_total = jnp.where(live_rows[None, None, :], total, 1.0)
    out_heads = jnp.where(live_rows[None, None, :, None], accum / safe_total[..., None], 0.0)
    attn_out = out_heads.transpose(2, 0, 1, 3).reshape(slots, heads_q, width).astype(jnp.bfloat16)
    log_norm = row_max + jnp.log(safe_total)
    out_four = attn_out.reshape(slots, heads_kv, context_group, width)
    delta = jnp.einsum("tgjc,tgjc->gjt", grad_four, out_four, preferred_element_type=jnp.float32)

    def tile_grads(both, group_id, block):
        mask, needed = tile_mask(group_id, block)
        key_block, value_block = block_pair(both, block)

        def tile_work(key_now):
            scores = scores_of(key_now)
            probs = jnp.where(mask, jnp.exp(scores - log_norm[..., None]), 0.0)
            probs_low = probs.astype(jnp.bfloat16)
            value_term = jnp.einsum(
                "gjtu,tgjc->ugc", probs_low, grad_four, preferred_element_type=jnp.float32
            )
            grad_probs = jnp.einsum(
                "tgjc,ugc->gjtu", grad_four, value_block, preferred_element_type=jnp.float32
            )
            grad_scores = (probs * (grad_probs - delta[..., None])).astype(jnp.bfloat16)
            query_term = jnp.einsum(
                "gjtu,ugc->tgjc", grad_scores, key_now, preferred_element_type=jnp.float32
            )
            key_term = (
                jnp.einsum(
                    "gjtu,tgjc->ugc", grad_scores, q_four, preferred_element_type=jnp.float32
                )
                * scale
            )
            key_term = lax.optimization_barrier(key_term.astype(jnp.bfloat16)).astype(jnp.float32)
            value_term = lax.optimization_barrier(value_term.astype(jnp.bfloat16)).astype(
                jnp.float32
            )
            return (query_term, key_term, value_term)

        def nothing(key_now):
            return (
                jnp.zeros((slots, heads_kv, context_group, width), jnp.float32),
                jnp.zeros((slots, heads_kv, width), jnp.float32),
                jnp.zeros((slots, heads_kv, width), jnp.float32),
            )

        return lax.cond(needed, tile_work, nothing, key_block)

    query_total = jnp.zeros((slots, heads_kv, context_group, width), jnp.float32)
    shares = []
    for both, group_id in rounds:

        def stack_step(block, carry, both=both, group_id=group_id):
            query_acc, key_stack, value_stack = carry
            query_term, key_term, value_term = tile_grads(both, group_id, block)
            key_stack = lax.dynamic_update_slice_in_dim(key_stack, key_term, block * slots, 0)
            value_stack = lax.dynamic_update_slice_in_dim(value_stack, value_term, block * slots, 0)
            return (query_acc + query_term, key_stack, value_stack)

        empty = jnp.zeros((inner_count * slots, heads_kv, width), jnp.float32)
        query_total, key_stack, value_stack = lax.fori_loop(
            0, inner_count, stack_step, (query_total, empty, empty)
        )
        shares.append(
            (
                lax.psum_scatter(
                    key_stack.astype(jnp.bfloat16), "inner", scatter_dimension=0, tiled=True
                ).astype(jnp.float32),
                lax.psum_scatter(
                    value_stack.astype(jnp.bfloat16), "inner", scatter_dimension=0, tiled=True
                ).astype(jnp.float32),
            )
        )
    returned = passed_along(as_sent(shares[1]), "outer", -1)
    key_gradient = (shares[0][0] + returned[0]).astype(jnp.bfloat16)
    value_gradient = (shares[0][1] + returned[1]).astype(jnp.bfloat16)
    grad_queries = (query_total * scale).reshape(slots, heads_q, width).astype(jnp.bfloat16)
    return (attn_out, grad_queries, key_gradient, value_gradient)


def solution(mesh):
    in_specs = (
        P(("outer", "inner"), None, None),
        P(("outer", "inner"), None, None),
        P(("outer", "inner"), None, None),
        P(("outer", "inner"), None, None),
        P(),
        P(),
    )
    out_specs = (
        P(("outer", "inner"), None, None),
        P(("outer", "inner"), None, None),
        P(("outer", "inner"), None, None),
        P(("outer", "inner"), None, None),
    )
    return jax.shard_map(
        on_device, mesh=mesh, in_specs=in_specs, out_specs=out_specs, check_vma=False
    )
```

profile of v0, /device:TPU:2, one launch (start us, length us, event | category | flops | bytes accessed | tf_op | source)
XLA Modules:
  0.0 942.2 jit_solution(17433742324010401054)
XLA Ops:
  13.9 9.0 collective-permute-done
  23.7 8.8 collective-permute-done.1
  36.0 13.5 %all-gather.5.cloned.1.call-done = bf16[2048,4,128]{2,0,1:T(8,128)(2,1)} async-done(((bf16[128,4,128]{2,0,1:T(8,128)(2,1)}), bf16[2048,4,128]{2,0,1:T(8,128)(2,1)}) %all-gather.5.cloned.1.call-update) | async-done | bytes 2097168 | tf_op jit(solution)/shard_map/all_gather | solution.py:55
  49.5 41.2 %all-gather.7.cloned.1.call-done = bf16[2048,4,128]{2,0,1:T(8,128)(2,1)} async-done(((bf16[128,4,128]{2,0,1:T(8,128)(2,1)}), bf16[2048,4,128]{2,0,1:T(8,128)(2,1)}) %all-gather.7.cloned.1.call-update) | async-done | bytes 2097168 | tf_op jit(solution)/shard_map/all_gather | solution.py:56
  92.3 114.6 %while.80 = (s32[]{:T(128)}, f32[4,8,128]{2,1,0:T(8,128)S(1)}, f32[4,8,128]{2,1,0:T(8,128)S(1)}, f32[4,8,128,128]{3,2,1,0:T(8,128)}, s32[]{:T(128)}, /*index=5*/...) while((s32[]{:T(128)}, f32[4,8,128]{2,1,0:T(8,128)S(1)}, ...), condition=%wide.region_5.6_spmd.clone, body=%wide.region_0.5_spmd.clone.sunk | while | flops 275341312 | bytes 29164556 | solution.py:105
  94.1 5.7 conditional.12
  109.2 5.7 conditional.12
  116.7 5.7 conditional.12
  124.2 5.7 conditional.12
  131.7 5.7 conditional.12
  141.1 5.7 conditional.12
  148.6 5.7 conditional.12
  156.1 5.7 conditional.12
  163.6 5.7 conditional.12
  171.2 5.7 conditional.12
  178.7 5.7 conditional.12
  193.7 5.7 conditional.12
  201.2 5.7 conditional.12
  206.9 114.9 %while.81 = (s32[]{:T(128)}, f32[4,8,128]{2,1,0:T(8,128)S(1)}, f32[4,8,128]{2,1,0:T(8,128)S(1)}, f32[4,8,128,128]{3,2,1,0:T(8,128)}, s32[]{:T(128)}, /*index=5*/...) while((s32[]{:T(128)}, f32[4,8,128]{2,1,0:T(8,128)S(1)}, ...), condition=%wide.region_11.12_spmd.clone, body=%wide.region_6.11_spmd.clone.sunk | while | flops 275341312 | bytes 29164556 | solution.py:105
  208.8 5.7 conditional.13
  216.3 5.7 conditional.13
  231.4 5.7 conditional.13
  238.9 5.7 conditional.13
  246.4 5.7 conditional.13
  261.5 5.7 conditional.13
  269.0 5.7 conditional.13
  276.6 5.7 conditional.13
  293.5 5.7 conditional.13
  301.0 5.7 conditional.13
  308.6 5.7 conditional.13
  316.1 5.7 conditional.13
  328.2 208.8 %while.83 = (s32[]{:T(128)}, f32[128,4,8,128]{3,0,2,1:T(8,128)}, bf16[2048,4,128]{2,1,0:T(4,128)(2,1)}, bf16[2048,4,128]{2,1,0:T(4,128)(2,1)}, s32[]{:T(128)}, /...) while((s32[]{:T(128)}, f32[128,4,8,128]{3,0,2,1:T(8,128)}, ...), condition=%wide.region_15.16_spmd.clone, body=%wide.region_12.15_spmd.clone.sunk | while | flops 676085760 | bytes 23530464 | solution.py:165
  330.1 6.6 conditional.15
  342.8 6.6 conditional.15
  356.2 6.6 conditional.15
  369.6 6.6 conditional.15
  383.0 6.6 conditional.15
  396.4 6.6 conditional.15
  418.2 6.6 conditional.15
  431.6 6.6 conditional.15
  445.0 6.6 conditional.15
  458.4 6.6 conditional.15
  471.8 6.6 conditional.15
  485.2 6.6 conditional.15
  498.6 6.6 conditional.15
  512.0 6.6 conditional.15
  525.4 6.6 conditional.15
  540.2 209.5 %while.82 = (s32[]{:T(128)}, f32[128,4,8,128]{3,0,2,1:T(8,128)}, bf16[2048,4,128]{2,1,0:T(4,128)(2,1)}, bf16[2048,4,128]{2,1,0:T(4,128)(2,1)}, s32[]{:T(128)}, /...) while((s32[]{:T(128)}, f32[128,4,8,128]{3,0,2,1:T(8,128)}, ...), condition=%wide.region_19.20_spmd.clone, body=%wide.region_16.19_spmd.clone.sunk | while | flops 675561472 | bytes 23530452 | solution.py:165
  542.1 6.7 conditional.14
  555.5 6.7 conditional.14
  568.9 6.7 conditional.14
  582.3 6.7 conditional.14
  595.7 6.7 conditional.14
  609.1 6.7 conditional.14
  622.5 6.7 conditional.14
  635.9 6.7 conditional.14
  649.3 6.7 conditional.14
  662.7 6.7 conditional.14
  676.1 6.7 conditional.14
  698.0 6.7 conditional.14
  711.4 6.7 conditional.14
  724.8 6.7 conditional.14
  738.2 6.7 conditional.14
  753.0 163.2 %all-reduce.7.cloned.1.call-done = (bf16[2048,4,128]{2,1,0:T(4,128)(2,1)}, bf16[2048,4,128]{2,1,0:T(4,128)(2,1)}, bf16[2048,4,128]{2,1,0:T(4,128)(2,1)}, bf16[2048,4,128]{2,1,0:T(4,128)(2,1)}) async-done(((bf16[2048,4,128]{2,1,0:T(4,128)(2,1)}, bf16[2048,4,128]{2,1,0:T(4,128)(2,1)}, bf16[2048,4,128]{2,1,0:T(4,128)(2,1)}, bf16[2048,4,128]{2,1,0:T(4,128)(2,1)}), (bf16[2048,4,128]{2,1,0:T(4,128)(2,1)}, ...) | async-done | bytes 8388624
  (899 shorter events, 640.6 us)
Async XLA Ops:
  7.2 27.8 %copy-start.5 = (bf16[128,32,128]{2,1,0:T(8,128)(2,1)S(1)}, bf16[128,32,128]{2,1,0:T(8,128)(2,1)}, u32[]{:S(2)}) copy-start(bf16[128,32,128]{2,1,0:T(8,128)(2,1)} %param.25) | copy-start | bytes 3145732
  7.2 42.3 %all-gather.5.cloned.1.call-start = ((), (), s32[]{:S(2)}) async-start(), calls=%async_computation | async-start | bytes 2228224 | tf_op jit(solution)/shard_map/all_gather | solution.py:55
  8.9 81.8 %all-gather.7.cloned.1.call-start = ((), (), s32[]{:S(2)}) async-start(), calls=%async_computation.1 | async-start | bytes 2228224 | tf_op jit(solution)/shard_map/all_gather | solution.py:56
  10.6 196.4 %all-gather.9.cloned.1.call-start = ((), (), s32[]{:S(2)}) async-start(), calls=%async_computation.2 | async-start | bytes 2228224 | tf_op jit(solution)/shard_map/all_gather | solution.py:55
  10.6 12.3 %collective-permute-start = (bf16[128,4,128]{2,0,1:T(8,128)(2,1)}, bf16[128,4,128]{2,0,1:T(8,128)(2,1)S(1)}, u32[]{:S(2)}, u32[]{:S(2)}) collective-permute-start(bf16[128,4,128]{2,0,1:T(8,128)(2,1)} %copy.30), channel_id=1, source_target_pairs={{240,0},{0,16},{16,32},{32,48},{48,64},{64,80},{80,96},{96,112},{1... | collective-permute-start | bytes 393224 | tf_op jit(solution)/shard_map/ppermute | solution.py:15
  23.6 183.4 %all-gather.11.cloned.1.call-start = ((), (), s32[]{:S(2)}) async-start(), calls=%async_computation.3 | async-start | bytes 2228224 | tf_op jit(solution)/shard_map/all_gather | solution.py:56
  23.6 8.9 collective-permute-start.1
  33.2 883.0 %all-reduce.7.cloned.1.call-start = ((), (), s32[]{:S(2)}) async-start(), calls=%async_computation.4 | async-start | bytes 16777216
  33.2 2.1 copy-start.10
  33.2 2.7 copy-start.7
  94.3 2.1 copy-start
  98.5 1.4 copy-start.1
  101.8 2.0 copy-start
  106.0 1.4 copy-start.1
  109.3 2.1 copy-start
  113.5 1.4 copy-start.1
  116.8 2.1 copy-start
  121.0 1.4 copy-start.1
  124.3 2.1 copy-start
  128.6 1.4 copy-start.1
  131.9 2.0 copy-start
  136.1 1.4 copy-start.1
  141.2 2.0 copy-start
  145.4 1.4 copy-start.1
  148.7 2.1 copy-start
  153.0 1.4 copy-start.1
  156.3 2.1 copy-start
  160.5 1.4 copy-start.1
  163.8 2.1 copy-start
  168.0 1.4 copy-start.1
  171.3 2.1 copy-start
  178.8 2.1 copy-start
  186.3 2.0 copy-start
  190.5 1.4 copy-start.1
  193.8 2.1 copy-start
  198.1 1.4 copy-start.1
  201.4 2.1 copy-start
  208.9 2.1 copy-start.2
  216.4 2.1 copy-start.2
  220.7 1.4 copy-start.3
  224.0 2.0 copy-start.2
  228.2 1.4 copy-start.3
  231.5 2.1 copy-start.2
  239.0 2.1 copy-start.2
  246.6 2.1 copy-start.2
  254.1 2.0 copy-start.2
  261.6 2.1 copy-start.2
  269.2 2.1 copy-start.2
  273.4 1.4 copy-start.3
  276.7 2.1 copy-start.2
  280.9 1.4 copy-start.3
  284.2 2.0 copy-start.2
  288.5 1.4 copy-start.3
  293.7 2.0 copy-start.2
  301.2 2.1 copy-start.2
  305.4 1.4 copy-start.3
  308.7 2.1 copy-start.2
  312.9 1.4 copy-start.3
  316.3 2.1 copy-start.2
  320.5 1.4 copy-start.3
  749.8 1.9 copy-start.4
  749.8 172.9 %copy-start.6 = (bf16[4,8,128,128]{3,2,1,0:T(8,128)(2,1)S(1)}, bf16[4,8,128,128]{3,2,1,0:T(8,128)(2,1)}, u32[]{:S(2)}) copy-start(bf16[4,8,128,128]{3,2,1,0:T(8,128)(2,1)} %get-tuple-element.2340) | copy-start | bytes 3145732
  917.1 11.3 %collective-permute-start.2 = (bf16[128,4,128]{2,1,0:T(4,128)(2,1)S(1)}, bf16[128,4,128]{2,1,0:T(4,128)(2,1)S(1)}, u32[]{:S(2)}, u32[]{:S(2)}) collective-permute-start(bf16[128,4,128]{2,1,0:T(4,128)(2,1)S(1)} %constant_dynamic-slice_fusion.1), channel_id=1, source_target_pairs={{16,0},{32,16},{48,32},{64,48},{80,64},{96,80},{112,96},{128,112},... | collective-permute-start | bytes 393224 | tf_op jit(solution)/shard_map/ppermute | solution.py:15
  927.5 6.5 collective-permute-start.3
  (13 other events, 15.5 us)
Sparse Core Ops, SparseCore 0:
  10.4 39.0 all-gather.4
  51.9 38.7 all-gather.6
  93.1 36.4 all-gather.8
  131.9 36.6 all-gather.10
  749.9 166.2 all-reduce.6
where the time goes:
time: 950 us; the launch traced here: 942 us
  matrix products  305 us (32%)
  waiting for transfers between devices  240 us (25%)
  other arithmetic  155 us (16%)
  local copies, waits for them, and re-layouts  135 us (14%)
  loops' own time  83.2 us (9%)
  between operations  14.6 us (2%)
  starting transfers between devices  9.99 us (1%)
    unnamed x6, waiting for transfers between devices  163 us
    add x32, other arithmetic, stack_step(): return (query_acc + query_term, key_stack, value_stack)  127 us
    dot_general x60, matrix products, scores_of(): jnp.einsum('tgjc,ugc->gjtu', q_four, key_block, preferred_element_type=jn...  89.3 us
    dot_general x30, matrix products, tile_work(): jnp.einsum('gjtu,ugc->tgjc', grad_scores, key_now, preferred_element_type...  83.7 us
    dot_general x30, matrix products, forward_work(): jnp.einsum('gjtu,ugc->gjtc', weights.astype(jnp.bfloat16), value_block, p...  64.6 us
    all_gather x2, waiting for transfers between devices, collect_group(): lax.all_gather(both[1], 'inner', axis=0, tiled=True)  41.2 us
    dot_general x30, matrix products, tile_work(): jnp.einsum('tgjc,ugc->gjtu', grad_four, value_block, preferred_element_ty...  41.1 us
    cond x150, local copies, waits for them, and re-layouts  40.7 us
  transfers between devices with their start and end apart: 9, of which 6 were waited for; matrix products, arithmetic and copies ran while one was open for 9% of the time, Pallas kernels for 0%

commit v1 on v0

v1 whole, which is shorter than its diff:
```python
import functools
import math

import jax
import jax.numpy as jnp
from jax import lax
from jax.experimental import pallas as pl
from jax.experimental.pallas import tpu as pltpu
from jax.sharding import Mesh
from jax.sharding import PartitionSpec as P

REGION = 1024
SLOTS = 128
WIDTH = 128
HEADS_Q = 32
HEADS_KV = 4
N_OUTER = 16
N_Y = 2
N_X = 4
N_CORE = 2
WINDOW = 32
KEY_ROWS = WINDOW * SLOTS
PIECES = 8

QUERY_AXES = ("x", "core")
SHARDS = N_X * N_CORE
HEADS = HEADS_Q // SHARDS
QUERY_ROWS = SHARDS * SLOTS
TILES = SHARDS
LANES = HEADS * SLOTS
UNIT = 256
SPAN = 512
UNITS = KEY_ROWS // UNIT

FILL = -1e30
FLOOR = -1e29
SCALE = WIDTH ** (-0.5)
BASE_TWO = SCALE * math.log2(math.e)
BF16, F32, I32 = jnp.bfloat16, jnp.float32, jnp.int32

KEY_ORDER = 0
KEY_OFFSET = 32
KEY_COUNT = 64
QUERY_ORDER = 96
QUERY_OFFSET = 112
QUERY_COUNT = 128
QUERY_KEY = 144
REACH = 160
CLEAR = 176
TILE_COUNT = 192
SCALARS = 193


def slots():
    return lax.broadcasted_iota(I32, (SLOTS, WIDTH), 0)


def up(n, unit):
    return (n + unit - 1) // unit


def tile_rows(i):
    return pl.ds(pl.multiple_of(i * SLOTS, SLOTS), SLOTS)


def unit_rows(u, rows):
    return pl.ds(pl.multiple_of(u * UNIT, UNIT), rows)


def pack_rows(sc, array, packed):
    slot = slots()
    packed[:, tile_rows(sc[TILE_COUNT] - 1), :] = jnp.zeros((HEADS, SLOTS, WIDTH), F32)

    @pl.loop(0, SHARDS)
    def _(j):
        s = sc[QUERY_ORDER + j]
        live = (slot < sc[QUERY_COUNT + s])[None]
        packed[:, pl.ds(sc[QUERY_OFFSET + s], SLOTS), :] = jnp.where(live, array[s].astype(F32), 0.0)


def unpack_rows(sc, packed, array):
    slot = slots()

    @pl.loop(0, SHARDS)
    def _(s):
        live = (slot < sc[QUERY_COUNT + s])[None]
        rows = packed[:, pl.ds(sc[QUERY_OFFSET + s], SLOTS), :]
        array[s] = jnp.where(live, rows, 0.0).astype(BF16)


def shown(s, unit, limit):
    place = lax.broadcasted_iota(I32, s.shape, 0)
    return jnp.where(place <= limit - unit * UNIT, s, FILL)


def over_keys(sc, i, step, carry):
    clear = sc[CLEAR + i]
    carry = lax.fori_loop(
        0, clear, lambda n, c: step(n * (SPAN // UNIT), SPAN // UNIT, False, c), carry
    )
    return lax.fori_loop(
        clear * (SPAN // UNIT), up(sc[REACH + i], UNIT), lambda u, c: step(u, 1, True, c), carry
    )


def fold(op, s):
    return op(s.reshape(-1, 8, s.shape[1]), axis=0)


def turned(ref, u, units):
    return jnp.concatenate([ref[u + n] for n in range(units)], axis=1)


def forward(sc, q_ref, *refs):
    pieces, rest = refs[:PIECES], refs[PIECES:]
    o_ref, oc, qc, kc, vc, kt, norm_ref, limit_ref, stage, kf, vf, vt, qf, of, thr, scr = rest
    slot = slots()
    tiles = sc[TILE_COUNT]
    most = sc[REACH + tiles - 1]
    for p, ref in enumerate(pieces):
        stage[p * N_X : (p + 1) * N_X] = ref[...]
    tail = unit_rows(up(most, UNIT) - 1, UNIT)
    kf[tail, :] = jnp.zeros((UNIT, WIDTH), F32)
    vf[tail, :] = jnp.zeros((UNIT, WIDTH), F32)

    @pl.loop(0, WINDOW)
    def _(j):
        w = sc[KEY_ORDER + j]
        rows = pl.ds(sc[KEY_OFFSET + w], SLOTS)
        kf[rows, :] = stage[w, 0].astype(F32)
        vf[rows, :] = stage[w, 1].astype(F32)

    @pl.loop(0, up(most, UNIT))
    def _(u):
        rows = unit_rows(u, UNIT)
        keys = kf[rows, :].astype(BF16)
        vals = vf[rows, :].astype(BF16)
        kc[rows, :] = keys
        vc[rows, :] = vals
        kt[u] = keys.T
        vt[u] = vals.T

    thr[tile_rows(tiles - 1), :] = jnp.full((SLOTS, WIDTH), -1, I32)

    @pl.loop(0, SHARDS)
    def _(j):
        s = sc[QUERY_ORDER + j]
        thr[pl.ds(sc[QUERY_OFFSET + s], SLOTS), :] = jnp.where(
            slot < sc[QUERY_COUNT + s], slot + sc[QUERY_KEY + s], -1
        )

    pack_rows(sc, q_ref, qf)

    @pl.loop(0, tiles)
    def _(i):
        rows = tile_rows(i)
        limit = jnp.concatenate([thr[rows, :].T[0:1, :]] * HEADS, axis=1)
        limit_ref[i] = limit
        q_tile = qf[:, rows, :].astype(BF16)
        qc[:, rows, :] = q_tile
        q_turn = q_tile.reshape(LANES, WIDTH).T

        def score(u, units, masked, top):
            s = jnp.dot(kc[unit_rows(u, units * UNIT), :], q_turn, preferred_element_type=F32)
            if masked:
                s = shown(s, u, limit)
            scr[unit_rows(u, units * UNIT), :] = s
            return jnp.maximum(top, fold(jnp.max, s))

        top = over_keys(sc, i, score, jnp.full((8, LANES), FLOOR, F32))
        top = jnp.max(top, axis=0, keepdims=True) * BASE_TWO

        def weigh(u, units, masked, carry):
            total, acc = carry
            w = jnp.exp2(scr[unit_rows(u, units * UNIT), :] * BASE_TWO - top)
            total = total + fold(jnp.sum, w)
            acc = acc + jnp.dot(turned(vt, u, units), w.astype(BF16), preferred_element_type=F32)
            return total, acc

        total, acc = over_keys(
            sc, i, weigh, (jnp.zeros((8, LANES), F32), jnp.zeros((WIDTH, LANES), F32))
        )
        total = jnp.sum(total, axis=0, keepdims=True)
        total = jnp.where(total > 0.0, total, 1.0)
        norm_ref[i] = top + jnp.log2(total)
        out = (acc * (1.0 / total)).T.reshape(HEADS, SLOTS, WIDTH)
        of[:, rows, :] = out
        oc[:, rows, :] = out.astype(BF16)

    unpack_rows(sc, of, o_ref)


def backward(sc, g_ref, oc, qc, kc, vc, kt, norm_ref, limit_ref, dq_ref, near_ref, far_ref, gf, dqf, dk, dv):
    @pl.loop(0, UNITS)
    def _(u):
        dk[unit_rows(u, UNIT), :] = jnp.zeros((UNIT, WIDTH), F32)
        dv[unit_rows(u, UNIT), :] = jnp.zeros((UNIT, WIDTH), F32)

    pack_rows(sc, g_ref, gf)

    @pl.loop(0, sc[TILE_COUNT])
    def _(i):
        rows = tile_rows(i)
        limit = limit_ref[i]
        norm = norm_ref[i]
        q_tile = qc[:, rows, :].reshape(LANES, WIDTH)
        g_tile = gf[:, rows, :].astype(BF16).reshape(LANES, WIDTH)
        q_turn = q_tile.T
        g_turn = g_tile.T
        o_turn = oc[:, rows, :].reshape(LANES, WIDTH).T
        delta = jnp.sum(g_turn.astype(F32) * o_turn.astype(F32), axis=0, keepdims=True)

        def step(u, units, masked, acc):
            at = unit_rows(u, units * UNIT)
            s = jnp.dot(kc[at, :], q_turn, preferred_element_type=F32)
            dp = jnp.dot(vc[at, :], g_turn, preferred_element_type=F32)
            if masked:
                s = shown(s, u, limit)
            p = jnp.exp2(s * BASE_TWO - norm)
            ds = (p * (dp - delta)).astype(BF16)
            dv[at, :] += jnp.dot(p.astype(BF16), g_tile, preferred_element_type=F32)
            dk[at, :] += jnp.dot(ds, q_tile, preferred_element_type=F32)
            return acc + jnp.dot(turned(kt, u, units), ds, preferred_element_type=F32)

        acc = over_keys(sc, i, step, jnp.zeros((WIDTH, LANES), F32))
        dqf[:, rows, :] = (acc * SCALE).T.reshape(HEADS, SLOTS, WIDTH)

    unpack_rows(sc, dqf, dq_ref)
    slot = slots()
    for g in range(2):
        for far in range(2):
            ref = far_ref if far else near_ref

            @pl.loop(0, 2 * N_X)
            def _(e, g=g, far=far, ref=ref):
                y, x = e // N_X, e % N_X
                w = g * 16 + far * 8 + e
                rows = pl.ds(sc[KEY_OFFSET + w], SLOTS)
                live = slot < sc[KEY_COUNT + w]
                ref[g, y, x, 0] = jnp.where(live, dk[rows, :] * SCALE, 0.0).astype(BF16)
                ref[g, y, x, 1] = jnp.where(live, dv[rows, :], 0.0).astype(BF16)


ROWS = (SHARDS, HEADS, SLOTS, WIDTH)
PACKED_ROWS = (HEADS, QUERY_ROWS, WIDTH)
PACKING_ROWS = pltpu.VMEM((HEADS, QUERY_ROWS + SLOTS, WIDTH), F32)
PACKING_KEYS = pltpu.VMEM((KEY_ROWS + SLOTS, WIDTH), F32)


def call(kernel, operands, out_shape, scratch, matmuls, name):
    vmem = pl.BlockSpec(memory_space=pltpu.VMEM)
    pairs = LANES * QUERY_ROWS // SLOTS * KEY_ROWS // 6
    return pl.pallas_call(
        kernel,
        out_shape=out_shape,
        in_specs=[pl.BlockSpec(memory_space=pltpu.SMEM)] + [vmem] * (len(operands) - 1),
        out_specs=(vmem,) * len(out_shape),
        scratch_shapes=scratch,
        compiler_params=pltpu.CompilerParams(vmem_limit_bytes=56 * 1024 * 1024),
        cost_estimate=pl.CostEstimate(
            flops=matmuls * 2 * pairs * WIDTH, bytes_accessed=8 << 20, transcendentals=pairs
        ),
        name=name,
    )(*operands)


def run_forward(scalars, q, pieces):
    shape = jax.ShapeDtypeStruct
    turned_keys = (UNITS, WIDTH, UNIT)
    o, *packed = call(
        forward,
        (scalars, q, *pieces),
        (
            shape(ROWS, BF16),
            shape(PACKED_ROWS, BF16),
            shape(PACKED_ROWS, BF16),
            shape((KEY_ROWS, WIDTH), BF16),
            shape((KEY_ROWS, WIDTH), BF16),
            shape(turned_keys, BF16),
            shape((TILES, 1, LANES), F32),
            shape((TILES, 1, LANES), I32),
        ),
        [
            pltpu.VMEM((WINDOW, 2, SLOTS, WIDTH), BF16),
            PACKING_KEYS,
            PACKING_KEYS,
            pltpu.VMEM(turned_keys, BF16),
            PACKING_ROWS,
            PACKING_ROWS,
            pltpu.VMEM((QUERY_ROWS + SLOTS, WIDTH), I32),
            pltpu.VMEM((KEY_ROWS, LANES), F32),
        ],
        2,
        "window_forward",
    )
    return o, packed


def run_backward(scalars, g, packed):
    terms = jax.ShapeDtypeStruct((2, 2, N_X, 2, SLOTS, WIDTH), BF16)
    return call(
        backward,
        (scalars, g, *packed),
        (jax.ShapeDtypeStruct(ROWS, BF16), terms, terms),
        [PACKING_ROWS, PACKING_ROWS, PACKING_KEYS, PACKING_KEYS],
        5,
        "window_backward",
    )


def plan(kept_offset, region_pos):
    outer, y, x_, core = (lax.axis_index(a) for a in ("outer", "y", "x", "core"))
    shard = jnp.arange(N_OUTER * N_Y * N_X * N_CORE)
    counts = jnp.sum((kept_offset < REGION).astype(jnp.int32), axis=1)

    def pick(ids):
        hit = ids[:, None] == shard[None, :]
        of = lambda a: jnp.sum(jnp.where(hit, a[None, :], 0), axis=1)
        return of(counts), of(region_pos)

    w = jnp.arange(WINDOW)
    g, p, x = w // 16, w // 4 % 4, (x_ - w) % 4
    group = jnp.where(g == 0, outer, (outer - 1) % N_OUTER)
    count, place = pick(
        group * 16 + ((y ^ (p % 2)) * N_X + x) * N_CORE + (core ^ (p // 2))
    )
    before = place[None, :] < place[:, None]
    offset = jnp.sum(jnp.where(before, count[None, :], 0), axis=1)
    rank = jnp.sum(before.astype(jnp.int32), axis=1)
    order = jnp.sum(jnp.where(rank[None, :] == w[:, None], w[None, :], 0), axis=1)

    s = jnp.arange(SHARDS)
    q_count, q_place = pick(outer * 16 + (y * N_X + s // 2) * N_CORE + s % 2)
    q_before = q_place[None, :] < q_place[:, None]
    q_offset = jnp.sum(jnp.where(q_before, q_count[None, :], 0), axis=1)
    q_rank = jnp.sum(q_before.astype(jnp.int32), axis=1)
    q_order = jnp.sum(jnp.where(q_rank[None, :] == s[:, None], s[None, :], 0), axis=1)
    q_key = jnp.sum(jnp.where(place[None, :] < q_place[:, None], count[None, :], 0), axis=1)

    start = jnp.arange(TILES)[:, None] * SLOTS
    within = (q_offset[None, :] < start + SLOTS) & (q_offset[None, :] + q_count[None, :] > start)
    end = q_key[None, :] + jnp.minimum(q_count[None, :], start + SLOTS - q_offset[None, :])
    reach = jnp.max(jnp.where(within, end, 0), axis=1)
    first = q_key[None, :] + jnp.maximum(start - q_offset[None, :], 0)
    clear = (jnp.min(jnp.where(within, first, KEY_ROWS), axis=1) + 1) // SPAN
    tiles = (jnp.sum(q_count) + SLOTS - 1) // SLOTS

    pad = lambda a, n: jnp.pad(a, (0, n - a.shape[0]))
    return jnp.concatenate([
        order, offset, count,
        pad(q_order, 16), pad(q_offset, 16), pad(q_count, 16), pad(q_key, 16), pad(reach, 16),
        pad(clear, 16),
        tiles[None],
    ]).astype(jnp.int32)


def total(*parts):
    return functools.reduce(jnp.add, [a.astype(F32) for a in parts]).astype(BF16)


def to_x(block, step):
    return lax.ppermute(block, "x", [(i, (i + step) % N_X) for i in range(N_X)])


def to_core(block):
    return lax.ppermute(block, "core", [(0, 1), (1, 0)])


def to_group(block, step, flip):
    route = [
        (i * 2 + y, (i + step) % N_OUTER * 2 + (y ^ flip))
        for i in range(N_OUTER)
        for y in range(N_Y)
    ]
    return lax.ppermute(block, ("outer", "y"), route)


def on_device(queries, keys, values, output_gradient, kept_offset, region_pos):
    x = lax.axis_index("x")
    exchange = functools.partial(lax.all_to_all, split_axis=0, concat_axis=0, tiled=True)
    scalars = plan(kept_offset, region_pos)

    kv = jnp.stack([keys, values]).transpose(2, 0, 1, 3)
    kv = [lax.dynamic_index_in_dim(kv, (x + k) % N_X, 0, keepdims=False) for k in range(N_X)]
    own = jnp.stack([to_x(kv[k], k) if k else kv[0] for k in range(N_X)])
    turned_queries, own = lax.optimization_barrier((queries.transpose(1, 0, 2), own))
    own_pair = (own, to_group(own, 0, 1))
    prev_pair = (to_group(own, 1, 0), to_group(own, 1, 1))
    pieces = (
        *own_pair, *(to_core(a) for a in own_pair), *prev_pair, *(to_core(a) for a in prev_pair)
    )

    q = exchange(turned_queries, QUERY_AXES).reshape(ROWS)
    gradient, q = lax.optimization_barrier((output_gradient.transpose(1, 0, 2), q))
    g = exchange(gradient, QUERY_AXES).reshape(ROWS)

    o, packed = run_forward(scalars, q, pieces)
    o_home = exchange(o.reshape(HEADS_Q, SLOTS, WIDTH), QUERY_AXES)
    dq, near, far = run_backward(scalars, g, packed)

    o_home, dq, near, far = lax.optimization_barrier((o_home, dq, near, far))
    far = to_core(far)
    term = lambda g, y: total(near[g, y], far[g, y])
    sums = total(
        term(0, 0),
        to_group(term(0, 1), 0, 1),
        to_group(term(1, 0), -1, 0),
        to_group(term(1, 1), -1, 1),
    )
    grads = [to_x(sums[k], -k) if k else sums[0] for k in range(N_X)]
    grads = jnp.stack([lax.select_n((h - x) % N_X, *grads) for h in range(N_X)])
    dq_home = exchange(dq.reshape(HEADS_Q, SLOTS, WIDTH), QUERY_AXES)

    return (
        o_home.transpose(1, 0, 2),
        dq_home.transpose(1, 0, 2),
        grads[:, 0].transpose(1, 0, 2),
        grads[:, 1].transpose(1, 0, 2),
    )


def solution(mesh):
    devices = mesh.devices.reshape(N_OUTER, N_Y, N_X, N_CORE)
    split = Mesh(devices, ("outer", "y", "x", "core"))
    rows = P(("outer", "y", "x", "core"), None, None)
    return jax.shard_map(
        on_device,
        mesh=split,
        in_specs=(rows, rows, rows, rows, P(), P()),
        out_specs=(rows, rows, rows, rows),
        check_vma=False,
    )
```

time: 950 us -> 137 us (0.14)
  matrix products: 305 us -> 0 us
  waiting for transfers between devices: 240 us -> 24.7 us
  other arithmetic: 155 us -> 4.56 us
  local copies, waits for them, and re-layouts: 135 us -> 13.5 us
  loops' own time: 83.2 us -> 0 us
  starting transfers between devices: 9.99 us -> 57.7 us
  Pallas kernels: 0 us -> 34.6 us
  between operations: 14.6 us -> 1.71 us
    dot_general x210 -> x0, matrix products: 305 us -> none  [the longest x60 89.3 us: scores_of(): jnp.einsum('tgjc,ugc->gjtu', q_four, key_block, preferred_element_type=jn...]
    unnamed x6 -> x0, waiting for transfers between devices: 163 us -> none
    add x63 -> x4, other arithmetic: 127 us -> 0.03 us  [the longest x1 0.02 us: plan(): group * 16 + ((y ^ p % 2) * N_X + x) * N_CORE + (core ^ p // 2)]
    another operation x68 -> x0, loops' own time: 83.2 us -> none  [the longest x2 39.6 us: on_device(): lax.fori_loop(0, inner_count, stack_step, (query_total, empty, empty))]
    all_gather x4 -> x0, waiting for transfers between devices: 54.7 us -> none  [the longest x2 41.2 us: collect_group(): lax.all_gather(both[1], 'inner', axis=0, tiled=True)]
    cond x150 -> x0, local copies, waits for them, and re-layouts: 40.7 us -> none
    dynamic_slice x65 -> x0, local copies, waits for them, and re-layouts: 38 us -> none  [the longest x64 37.4 us: tile_mask(): place = lax.dynamic_index_in_dim(region_pos, source, 0, keepdims=False)]
    pallas_call x0 -> x2, Pallas kernels: none -> 34.6 us  [call(): pl.pallas_call(kernel, out_shape=out_shape, in_specs=[pl.BlockSpec(memory...]
  transfers between devices with their start and end apart: 9 -> 21, of which waited for: 6 -> 7; matrix products, arithmetic and copies ran while one was open for 9% -> 8% of each run, Pallas kernels for 0% -> 25%
where the time goes in v1:
time: 137 us
  starting transfers between devices  57.7 us (42%)
  Pallas kernels  34.6 us (25%)
  waiting for transfers between devices  24.7 us (18%)
  local copies, waits for them, and re-layouts  13.5 us (10%)
  other arithmetic  4.56 us (3%)
  between operations  1.71 us (1%)
    pallas_call x2, Pallas kernels, call(): pl.pallas_call(kernel, out_shape=out_shape, in_specs=[pl.BlockSpec(memory...  34.6 us
    ppermute x6, starting transfers between devices, to_group(): return lax.ppermute(block, ('outer', 'y'), route)  26 us
    ppermute x6, waiting for transfers between devices, to_group(): return lax.ppermute(block, ('outer', 'y'), route)  18.1 us
    unnamed x36, local copies, waits for them, and re-layouts  11.7 us
    ppermute x6, starting transfers between devices, to_x(): return lax.ppermute(block, 'x', [(i, (i + step) % N_X) for i in range(N_X)])  10.2 us
    all_to_all x1, starting transfers between devices, on_device(): q = exchange(turned_queries, QUERY_AXES).reshape(ROWS)  5.67 us
    all_to_all x1, waiting for transfers between devices, on_device(): q = exchange(turned_queries, QUERY_AXES).reshape(ROWS)  5.18 us
    all_to_all x1, starting transfers between devices, on_device(): dq_home = exchange(dq.reshape(HEADS_Q, SLOTS, WIDTH), QUERY_AXES)  4.95 us
  transfers between devices with their start and end apart: 21, of which 7 were waited for; matrix products, arithmetic and copies ran while one was open for 8% of the time, Pallas kernels for 25%

profile of v1, /device:TPU:2, one launch (start us, length us, event | category | flops | bytes accessed | tf_op | source)
XLA Modules:
  0.0 136.6 jit_solution(4426855960024052987)
XLA Ops:
  0.7 1.1 copy_bitcast_fusion.2
  1.8 2.3 %collective-permute-start.2 = (bf16[2,128,128]{2,1,0:T(8,128)(2,1)S(1)}, bf16[2,128,128]{2,1,0:T(8,128)(2,1)S(1)}, u32[]{:S(2)}, u32[]{:S(2)}) collective-permute-start(bf16[2,128,128]{2,1,0:T(8,128)(2,1)S(1)} %get-tuple-element.84), channel_id=1, source_target_pairs={{0,6},{2,0},{4,2},{6,4},{1,7},{3,1},{5,3},{7,5},{8,14},{10,8},{12,... | collective-permute-start | bytes 196616 | tf_op jit(solution)/shard_map/ppermute | solution.py:362
  4.2 0.0 collective-permute-start
  4.2 3.1 %collective-permute-start.1 = (bf16[2,128,128]{2,1,0:T(8,128)(2,1)S(1)}, bf16[2,128,128]{2,1,0:T(8,128)(2,1)S(1)}, u32[]{:S(2)}, u32[]{:S(2)}) collective-permute-start(bf16[2,128,128]{2,1,0:T(8,128)(2,1)S(1)} %get-tuple-element.83), channel_id=1, source_target_pairs={{0,4},{2,6},{4,0},{6,2},{1,5},{3,7},{5,1},{7,3},{8,12},{10,14},{12... | collective-permute-start | bytes 196616 | tf_op jit(solution)/shard_map/ppermute | solution.py:362
  7.3 1.4 %copy.44 = bf16[128,32,128]{2,0,1:T(8,128)(2,1)} copy(bf16[128,32,128]{2,1,0:T(8,128)(2,1)S(1)} %copy-done) | data formatting | bytes 2097152 | tf_op args[0]
  8.6 0.0 collective-permute-done.2
  8.6 0.1 collective-permute-done
  8.7 1.2 collective-permute-done.1
  10.0 0.0 copy-start.1
  10.0 5.7 %all-to-all-start = ((bf16[32,128,128]{2,1,0:T(8,128)(2,1)}), bf16[32,128,128]{2,1,0:T(8,128)(2,1)S(1)}, u32[]{:S(2)}, u32[]{:S(2)}) async-start(bf16[32,128,128]{2,1,0:T(8,128)(2,1)} %bitcast.69), calls=%async_computation | async-start | bytes 2097152 | tf_op jit(solution)/shard_map/all_to_all | solution.py:393
  15.7 1.4 %copy.45 = bf16[128,32,128]{2,0,1:T(8,128)(2,1)} copy(bf16[128,32,128]{2,1,0:T(8,128)(2,1)S(1)} %copy-done.1) | data formatting | bytes 2097152 | tf_op args[3]
  17.1 0.0 copy-start.7
  17.1 0.1 convert_reduce_fusion
  17.2 0.6 copy-done.7
  17.8 0.7 select_reduce_fusion.3
  18.5 0.2 fusion.18
  18.7 0.2 select_reduce_fusion
  18.9 1.7 %collective-permute-start.3 = (bf16[4,2,128,128]{3,2,1,0:T(8,128)(2,1)S(1)}, bf16[4,2,128,128]{3,2,1,0:T(8,128)(2,1)S(1)}, u32[]{:S(2)}, u32[]{:S(2)}) collective-permute-start(bf16[4,2,128,128]{3,2,1,0:T(8,128)(2,1)S(1)} %pad_maximum_fusion.refs_0_), channel_id=1, source_target_pairs={{0,8},{8,0},{16,24},{24,16},{32,40},{40,32},{48,56},{56,48},{64,72... | collective-permute-start | bytes 786440 | tf_op jit(solution)/shard_map/ppermute | solution.py:375
  20.5 2.9 %collective-permute-start.6 = (bf16[4,2,128,128]{3,2,1,0:T(8,128)(2,1)S(1)}, bf16[4,2,128,128]{3,2,1,0:T(8,128)(2,1)S(1)}, u32[]{:S(2)}, u32[]{:S(2)}) collective-permute-start(bf16[4,2,128,128]{3,2,1,0:T(8,128)(2,1)S(1)} %pad_maximum_fusion.refs_0_), channel_id=1, source_target_pairs={{0,16},{8,24},{16,32},{24,40},{32,48},{40,56},{48,64},{56,72},{64,... | collective-permute-start | bytes 786440 | tf_op jit(solution)/shard_map/ppermute | solution.py:375
  23.4 1.6 %collective-permute-start.7 = (bf16[4,2,128,128]{3,2,1,0:T(8,128)(2,1)S(1)}, bf16[4,2,128,128]{3,2,1,0:T(8,128)(2,1)S(1)}, u32[]{:S(2)}, u32[]{:S(2)}) collective-permute-start(bf16[4,2,128,128]{3,2,1,0:T(8,128)(2,1)S(1)} %pad_maximum_fusion.refs_0_), channel_id=1, source_target_pairs={{0,24},{8,16},{16,40},{24,32},{32,56},{40,48},{48,72},{56,64},{64,... | collective-permute-start | bytes 786440 | tf_op jit(solution)/shard_map/ppermute | solution.py:375
  25.0 5.2 %all-to-all-done = bf16[32,128,128]{2,1,0:T(8,128)(2,1)S(1)} async-done(((bf16[32,128,128]{2,1,0:T(8,128)(2,1)}), bf16[32,128,128]{2,1,0:T(8,128)(2,1)S(1)}, u32[]{:S(2)}, u32[]{:S(2)}) %all-to-all-start) | async-done | bytes 1048608 | tf_op jit(solution)/shard_map/all_to_all | solution.py:393
  30.2 1.0 copy-done.2
  31.2 4.9 %all-to-all-start.2 = ((bf16[32,128,128]{2,1,0:T(8,128)(2,1)}), bf16[32,128,128]{2,1,0:T(8,128)(2,1)S(1)}, u32[]{:S(2)}, u32[]{:S(2)}) async-start(bf16[32,128,128]{2,1,0:T(8,128)(2,1)} %bitcast.70), calls=%async_computation.2 | async-start | bytes 2097152 | tf_op jit(solution)/shard_map/all_to_all | solution.py:395
  36.1 0.2 select_reduce_fusion.8
  36.3 0.2 select_reduce_fusion.6
  36.5 0.2 collective-permute-start.4
  36.7 0.0 collective-permute-done.3.refs_1_
  36.8 0.4 collective-permute-start.5
  37.1 0.1 collective-permute-start.8
  37.3 3.5 %collective-permute-done.7.refs_5_ = bf16[4,2,128,128]{3,2,1,0:T(8,128)(2,1)S(1)} collective-permute-done((bf16[4,2,128,128]{3,2,1,0:T(8,128)(2,1)S(1)}, bf16[4,2,128,128]{3,2,1,0:T(8,128)(2,1)S(1)}, u32[]{:S(2)}, u32[]{:S(2)}) %collective-permute-start.7) | collective-permute-done | bytes 262176 | tf_op jit(solution)/shard_map/ppermute | solution.py:375
  40.8 0.0 collective-permute-start.9
  41.6 0.2 fusion.16
  41.8 0.1 select_reduce_fusion.2
  41.9 0.7 concatenate.3.sc
  42.6 0.0 collective-permute-done.4.refs_2_
  42.6 0.0 collective-permute-done.5.refs_3_
  42.6 0.0 collective-permute-done.9.refs_7_
  42.7 0.6 copy-done.11
  43.3 0.1 copy-done.12
  43.4 0.1 copy-done.13
  43.5 0.8 copy-done.14
  44.2 17.1 %window_forward.1 = (bf16[8,4,128,128]{3,2,1,0:T(8,128)(2,1)}, bf16[4,1024,128]{2,1,0:T(8,128)(2,1)}, bf16[4,1024,128]{2,1,0:T(8,128)(2,1)}, bf16[4096,128]{1,0:...) custom-call(s32[193]{0:T(256)} %concatenate.3.sc, ...), custom_call_target="tpu_custom_call" | custom-call | flops 1431655424 | bytes 8388608 | tf_op jit(solution)/shard_map/window_forward/pallas_call | solution.py:253
  61.4 0.0 copy-start.3
  61.4 1.0 copy-done.3
  62.3 4.9 %all-to-all-start.1 = ((bf16[32,128,128]{2,1,0:T(8,128)(2,1)}), bf16[32,128,128]{2,1,0:T(8,128)(2,1)S(1)}, u32[]{:S(2)}, u32[]{:S(2)}) async-start(bf16[32,128,128]{2,1,0:T(8,128)(2,1)} %bitcast.76), calls=%async_computation.1 | async-start | bytes 2097152 | tf_op jit(solution)/shard_map/all_to_all | solution.py:398
  67.2 17.5 %window_backward.1 = (bf16[8,4,128,128]{3,2,1,0:T(8,128)(2,1)}, bf16[2,2,4,2,128,128]{5,4,3,2,1,0:T(8,128)(2,1)}, bf16[2,2,4,2,128,128]{5,4,3,2,1,0:T(8,128)(2,1)}) custom-call(s32[193]{0:T(256)} %concatenate.3.sc, bf16[8,4,128,128]{3,2,1,0:T(8,128)(2,1)} %bitcast.75, bf16[4,1024,128]{2,1,0:T(8,128)(2,1)} %get-tuple-element.28.oc, ...), custom_call_target="tpu_custom_call" | custom-call | flops 3579138560 | bytes 8388608 | tf_op jit(solution)/shard_map/window_backward/pallas_call | solution.py:253
  84.7 0.0 all-to-all-done.1
  84.7 0.3 collective-permute-start.10
  84.9 4.9 %all-to-all-start.3 = ((bf16[32,128,128]{2,1,0:T(8,128)(2,1)}), bf16[32,128,128]{2,1,0:T(8,128)(2,1)S(1)}, u32[]{:S(2)}, u32[]{:S(2)}) async-start(bf16[32,128,128]{2,1,0:T(8,128)(2,1)} %bitcast.74), calls=%async_computation.3 | async-start | bytes 2097152 | tf_op jit(solution)/shard_map/all_to_all | solution.py:412
  89.9 1.3 fusion.4
  91.2 19.2 %collective-permute-start.11 = (bf16[4,2,128,128]{3,2,1,0:T(8,128)(2,1)S(1)}, bf16[4,2,128,128]{3,2,1,0:T(8,128)(2,1)S(1)}, u32[]{:S(2)}, u32[]{:S(2)}) collective-permute-start(bf16[4,2,128,128]{3,2,1,0:T(8,128)(2,1)S(1)} %get-tuple-element.69), channel_id=1, source_target_pairs={{0,8},{8,0},{16,24},{24,16},{32,40},{40,32},{48,56},{56,48},{64,72... | collective-permute-start | bytes 786440 | tf_op jit(solution)/shard_map/ppermute | solution.py:375
  110.5 0.7 collective-permute-start.12
  111.1 11.6 %collective-permute-done.11 = bf16[4,2,128,128]{3,2,1,0:T(8,128)(2,1)S(1)} collective-permute-done((bf16[4,2,128,128]{3,2,1,0:T(8,128)(2,1)S(1)}, bf16[4,2,128,128]{3,2,1,0:T(8,128)(2,1)S(1)}, u32[]{:S(2)}, u32[]{:S(2)}) %collective-permute-start.11) | collective-permute-done | bytes 262176 | tf_op jit(solution)/shard_map/ppermute | solution.py:375
  122.7 1.3 collective-permute-done.12
  124.0 1.7 %collective-permute-done.13 = bf16[4,2,128,128]{3,2,1,0:T(8,128)(2,1)S(1)} collective-permute-done((bf16[4,2,128,128]{3,2,1,0:T(8,128)(2,1)S(1)}, bf16[4,2,128,128]{3,2,1,0:T(8,128)(2,1)S(1)}, u32[]{:S(2)}, u32[]{:S(2)}) %collective-permute-start.13) | collective-permute-done | bytes 262176 | tf_op jit(solution)/shard_map/ppermute | solution.py:375
  125.8 1.1 fusion.2
  126.9 0.4 collective-permute-start.14
  127.3 2.6 %collective-permute-start.15 = (bf16[2,128,128]{2,1,0:T(8,128)(2,1)S(1)}, bf16[2,128,128]{2,1,0:T(8,128)(2,1)S(1)}, u32[]{:S(2)}, u32[]{:S(2)}) collective-permute-start(bf16[2,128,128]{2,1,0:T(8,128)(2,1)S(1)} %get-tuple-element.80), channel_id=1, source_target_pairs={{0,4},{2,6},{4,0},{6,2},{1,5},{3,7},{5,1},{7,3},{8,12},{10,14},{12... | collective-permute-start | bytes 196616 | tf_op jit(solution)/shard_map/ppermute | solution.py:362
  129.9 1.8 %collective-permute-start.16 = (bf16[2,128,128]{2,1,0:T(8,128)(2,1)S(1)}, bf16[2,128,128]{2,1,0:T(8,128)(2,1)S(1)}, u32[]{:S(2)}, u32[]{:S(2)}) collective-permute-start(bf16[2,128,128]{2,1,0:T(8,128)(2,1)S(1)} %get-tuple-element.79), channel_id=1, source_target_pairs={{0,2},{2,4},{4,6},{6,0},{1,3},{3,5},{5,7},{7,1},{8,10},{10,12},{12... | collective-permute-start | bytes 196616 | tf_op jit(solution)/shard_map/ppermute | solution.py:362
  131.7 1.6 %copy.36 = bf16[128,32,128]{2,1,0:T(8,128)(2,1)} copy(bf16[128,32,128]{2,0,1:T(8,128)(2,1)S(1)} %bitcast.71) | data formatting | bytes 2097152
  133.3 0.0 all-to-all-done.3
  133.3 1.6 %copy.37 = bf16[128,32,128]{2,1,0:T(8,128)(2,1)} copy(bf16[128,32,128]{2,0,1:T(8,128)(2,1)S(1)} %bitcast.72) | data formatting | bytes 2097152
  135.1 0.8 copy.38
  135.9 0.8 copy.39
  (46 shorter events, 0.3 us)
Async XLA Ops:
  0.6 6.6 %copy-start = (bf16[128,32,128]{2,1,0:T(8,128)(2,1)S(1)}, bf16[128,32,128]{2,1,0:T(8,128)(2,1)}, u32[]{:S(2)}) copy-start(bf16[128,32,128]{2,1,0:T(8,128)(2,1)} %param.6) | copy-start | bytes 3145732
  1.8 6.8 %collective-permute-start.2 = (bf16[2,128,128]{2,1,0:T(8,128)(2,1)S(1)}, bf16[2,128,128]{2,1,0:T(8,128)(2,1)S(1)}, u32[]{:S(2)}, u32[]{:S(2)}) collective-permute-start(bf16[2,128,128]{2,1,0:T(8,128)(2,1)S(1)} %get-tuple-element.84), channel_id=1, source_target_pairs={{0,6},{2,0},{4,2},{6,4},{1,7},{3,1},{5,3},{7,5},{8,14},{10,8},{12,... | collective-permute-start | bytes 196616 | tf_op jit(solution)/shard_map/ppermute | solution.py:362
  4.2 4.6 %collective-permute-start = (bf16[2,128,128]{2,1,0:T(8,128)(2,1)S(1)}, bf16[2,128,128]{2,1,0:T(8,128)(2,1)S(1)}, u32[]{:S(2)}, u32[]{:S(2)}) collective-permute-start(bf16[2,128,128]{2,1,0:T(8,128)(2,1)S(1)} %get-tuple-element.82), channel_id=1, source_target_pairs={{0,2},{2,4},{4,6},{6,0},{1,3},{3,5},{5,7},{7,1},{8,10},{10,12},{12... | collective-permute-start | bytes 196616 | tf_op jit(solution)/shard_map/ppermute | solution.py:362
  4.2 5.8 %collective-permute-start.1 = (bf16[2,128,128]{2,1,0:T(8,128)(2,1)S(1)}, bf16[2,128,128]{2,1,0:T(8,128)(2,1)S(1)}, u32[]{:S(2)}, u32[]{:S(2)}) collective-permute-start(bf16[2,128,128]{2,1,0:T(8,128)(2,1)S(1)} %get-tuple-element.83), channel_id=1, source_target_pairs={{0,4},{2,6},{4,0},{6,2},{1,5},{3,7},{5,1},{7,3},{8,12},{10,14},{12... | collective-permute-start | bytes 196616 | tf_op jit(solution)/shard_map/ppermute | solution.py:362
  10.0 26.5 %copy-start.5 = (bf16[4,2,128,128]{3,2,1,0:T(8,128)(2,1)}, bf16[4,2,128,128]{3,2,1,0:T(8,128)(2,1)S(1)}, u32[]{:S(2)}) copy-start(bf16[4,2,128,128]{3,2,1,0:T(8,128)(2,1)S(1)} %pad_maximum_fusion.refs_0_) | copy-start | bytes 786436
  10.0 5.7 %copy-start.1 = (bf16[128,32,128]{2,1,0:T(8,128)(2,1)S(1)}, bf16[128,32,128]{2,1,0:T(8,128)(2,1)}, u32[]{:S(2)}) copy-start(bf16[128,32,128]{2,1,0:T(8,128)(2,1)} %param.9) | copy-start | bytes 3145732
  10.0 20.2 %all-to-all-start = ((bf16[32,128,128]{2,1,0:T(8,128)(2,1)}), bf16[32,128,128]{2,1,0:T(8,128)(2,1)S(1)}, u32[]{:S(2)}, u32[]{:S(2)}) async-start(bf16[32,128,128]{2,1,0:T(8,128)(2,1)} %bitcast.69), calls=%async_computation | async-start | bytes 2097152 | tf_op jit(solution)/shard_map/all_to_all | solution.py:393
  15.7 1.4 %copy-start.6 = (s32[256,128]{1,0:T(8,128)S(1)}, s32[256,128]{1,0:T(8,128)}, u32[]{:S(2)}) copy-start(s32[256,128]{1,0:T(8,128)} %param.10) | copy-start | bytes 393220
  17.1 0.7 copy-start.7
  18.9 17.9 %collective-permute-start.3 = (bf16[4,2,128,128]{3,2,1,0:T(8,128)(2,1)S(1)}, bf16[4,2,128,128]{3,2,1,0:T(8,128)(2,1)S(1)}, u32[]{:S(2)}, u32[]{:S(2)}) collective-permute-start(bf16[4,2,128,128]{3,2,1,0:T(8,128)(2,1)S(1)} %pad_maximum_fusion.refs_0_), channel_id=1, source_target_pairs={{0,8},{8,0},{16,24},{24,16},{32,40},{40,32},{48,56},{56,48},{64,72... | collective-permute-start | bytes 786440 | tf_op jit(solution)/shard_map/ppermute | solution.py:375
  20.5 16.6 %collective-permute-start.6 = (bf16[4,2,128,128]{3,2,1,0:T(8,128)(2,1)S(1)}, bf16[4,2,128,128]{3,2,1,0:T(8,128)(2,1)S(1)}, u32[]{:S(2)}, u32[]{:S(2)}) collective-permute-start(bf16[4,2,128,128]{3,2,1,0:T(8,128)(2,1)S(1)} %pad_maximum_fusion.refs_0_), channel_id=1, source_target_pairs={{0,16},{8,24},{16,32},{24,40},{32,48},{40,56},{48,64},{56,72},{64,... | collective-permute-start | bytes 786440 | tf_op jit(solution)/shard_map/ppermute | solution.py:375
  23.4 17.3 %collective-permute-start.7 = (bf16[4,2,128,128]{3,2,1,0:T(8,128)(2,1)S(1)}, bf16[4,2,128,128]{3,2,1,0:T(8,128)(2,1)S(1)}, u32[]{:S(2)}, u32[]{:S(2)}) collective-permute-start(bf16[4,2,128,128]{3,2,1,0:T(8,128)(2,1)S(1)} %pad_maximum_fusion.refs_0_), channel_id=1, source_target_pairs={{0,24},{8,16},{16,40},{24,32},{32,56},{40,48},{48,72},{56,64},{64,... | collective-permute-start | bytes 786440 | tf_op jit(solution)/shard_map/ppermute | solution.py:375
  30.2 1.0 copy-start.2
  31.2 30.2 %all-to-all-start.2 = ((bf16[32,128,128]{2,1,0:T(8,128)(2,1)}), bf16[32,128,128]{2,1,0:T(8,128)(2,1)S(1)}, u32[]{:S(2)}, u32[]{:S(2)}) async-start(bf16[32,128,128]{2,1,0:T(8,128)(2,1)} %bitcast.70), calls=%async_computation.2 | async-start | bytes 2097152 | tf_op jit(solution)/shard_map/all_to_all | solution.py:395
  36.5 6.1 %collective-permute-start.4 = (bf16[4,2,128,128]{3,2,1,0:T(8,128)(2,1)S(1)}, bf16[4,2,128,128]{3,2,1,0:T(8,128)(2,1)S(1)}, u32[]{:S(2)}, u32[]{:S(2)}) collective-permute-start(bf16[4,2,128,128]{3,2,1,0:T(8,128)(2,1)S(1)} %pad_maximum_fusion.refs_0_), channel_id=1, source_target_pairs={{0,1},{1,0},{2,3},{3,2},{4,5},{5,4},{6,7},{7,6},{8,9},{9,8},{10,11... | collective-permute-start | bytes 786440 | tf_op jit(solution)/shard_map/ppermute | solution.py:366
  36.8 5.9 %copy-start.8 = (bf16[4,2,128,128]{3,2,1,0:T(8,128)(2,1)}, bf16[4,2,128,128]{3,2,1,0:T(8,128)(2,1)S(1)}, u32[]{:S(2)}) copy-start(bf16[4,2,128,128]{3,2,1,0:T(8,128)(2,1)S(1)} %collective-permute-done.3.refs_1_) | copy-start | bytes 786436
  36.8 5.8 %collective-permute-start.5 = (bf16[4,2,128,128]{3,2,1,0:T(8,128)(2,1)S(1)}, bf16[4,2,128,128]{3,2,1,0:T(8,128)(2,1)S(1)}, u32[]{:S(2)}, u32[]{:S(2)}) collective-permute-start(bf16[4,2,128,128]{3,2,1,0:T(8,128)(2,1)S(1)} %collective-permute-done.3.refs_1_), channel_id=1, source_target_pairs={{0,1},{1,0},{2,3},{3,2},{4,5},{5,4},{6,7},{7,6},{8,9},{9,8},{10,11... | collective-permute-start | bytes 786440 | tf_op jit(solution)/shard_map/ppermute | solution.py:366
  37.1 5.5 %copy-start.9 = (bf16[4,2,128,128]{3,2,1,0:T(8,128)(2,1)}, bf16[4,2,128,128]{3,2,1,0:T(8,128)(2,1)S(1)}, u32[]{:S(2)}) copy-start(bf16[4,2,128,128]{3,2,1,0:T(8,128)(2,1)S(1)} %collective-permute-done.6.refs_4_) | copy-start | bytes 786436
  37.1 5.5 %collective-permute-start.8 = (bf16[4,2,128,128]{3,2,1,0:T(8,128)(2,1)S(1)}, bf16[4,2,128,128]{3,2,1,0:T(8,128)(2,1)S(1)}, u32[]{:S(2)}, u32[]{:S(2)}) collective-permute-start(bf16[4,2,128,128]{3,2,1,0:T(8,128)(2,1)S(1)} %collective-permute-done.6.refs_4_), channel_id=1, source_target_pairs={{0,1},{1,0},{2,3},{3,2},{4,5},{5,4},{6,7},{7,6},{8,9},{9,8},{10,11... | collective-permute-start | bytes 786440 | tf_op jit(solution)/shard_map/ppermute | solution.py:366
  40.8 1.9 %copy-start.10 = (bf16[4,2,128,128]{3,2,1,0:T(8,128)(2,1)}, bf16[4,2,128,128]{3,2,1,0:T(8,128)(2,1)S(1)}, u32[]{:S(2)}) copy-start(bf16[4,2,128,128]{3,2,1,0:T(8,128)(2,1)S(1)} %collective-permute-done.7.refs_5_) | copy-start | bytes 786436
  40.8 1.8 %collective-permute-start.9 = (bf16[4,2,128,128]{3,2,1,0:T(8,128)(2,1)S(1)}, bf16[4,2,128,128]{3,2,1,0:T(8,128)(2,1)S(1)}, u32[]{:S(2)}, u32[]{:S(2)}) collective-permute-start(bf16[4,2,128,128]{3,2,1,0:T(8,128)(2,1)S(1)} %collective-permute-done.7.refs_5_), channel_id=1, source_target_pairs={{0,1},{1,0},{2,3},{3,2},{4,5},{5,4},{6,7},{7,6},{8,9},{9,8},{10,11... | collective-permute-start | bytes 786440 | tf_op jit(solution)/shard_map/ppermute | solution.py:366
  42.6 0.7 copy-start.11
  42.6 0.8 copy-start.12
  42.6 0.9 copy-start.13
  43.5 0.8 copy-start.14
  61.4 1.0 copy-start.3
  62.3 22.3 %all-to-all-start.1 = ((bf16[32,128,128]{2,1,0:T(8,128)(2,1)}), bf16[32,128,128]{2,1,0:T(8,128)(2,1)S(1)}, u32[]{:S(2)}, u32[]{:S(2)}) async-start(bf16[32,128,128]{2,1,0:T(8,128)(2,1)} %bitcast.76), calls=%async_computation.1 | async-start | bytes 2097152 | tf_op jit(solution)/shard_map/all_to_all | solution.py:398
  84.7 5.2 %collective-permute-start.10 = (bf16[2,2,4,2,128,128]{5,4,3,2,1,0:T(8,128)(2,1)}, bf16[2,2,4,2,128,128]{5,4,3,2,1,0:T(8,128)(2,1)}, u32[]{:S(2)}, u32[]{:S(2)}) collective-permute-start(bf16[2,2,4,2,128,128]{5,4,3,2,1,0:T(8,128)(2,1)} %get-tuple-element.41), channel_id=1, source_target_pairs={{0,1},{1,0},{2,3},{3,2},{4,5},{5,4},{6,7},{7,6},{8,9},{9,8},{10,11... | collective-permute-start | bytes 3145736 | tf_op jit(solution)/shard_map/ppermute | solution.py:366
  84.9 5.0 %copy-start.4 = (bf16[2,2,4,2,128,128]{5,4,3,2,1,0:T(8,128)(2,1)S(1)}, bf16[2,2,4,2,128,128]{5,4,3,2,1,0:T(8,128)(2,1)}, u32[]{:S(2)}) copy-start(bf16[2,2,4,2,128,128]{5,4,3,2,1,0:T(8,128)(2,1)} %get-tuple-element.40) | copy-start | bytes 3145732
  84.9 48.4 %all-to-all-start.3 = ((bf16[32,128,128]{2,1,0:T(8,128)(2,1)}), bf16[32,128,128]{2,1,0:T(8,128)(2,1)S(1)}, u32[]{:S(2)}, u32[]{:S(2)}) async-start(bf16[32,128,128]{2,1,0:T(8,128)(2,1)} %bitcast.74), calls=%async_computation.3 | async-start | bytes 2097152 | tf_op jit(solution)/shard_map/all_to_all | solution.py:412
  91.2 31.5 %collective-permute-start.11 = (bf16[4,2,128,128]{3,2,1,0:T(8,128)(2,1)S(1)}, bf16[4,2,128,128]{3,2,1,0:T(8,128)(2,1)S(1)}, u32[]{:S(2)}, u32[]{:S(2)}) collective-permute-start(bf16[4,2,128,128]{3,2,1,0:T(8,128)(2,1)S(1)} %get-tuple-element.69), channel_id=1, source_target_pairs={{0,8},{8,0},{16,24},{24,16},{32,40},{40,32},{48,56},{56,48},{64,72... | collective-permute-start | bytes 786440 | tf_op jit(solution)/shard_map/ppermute | solution.py:375
  110.5 13.6 %collective-permute-start.12 = (bf16[4,2,128,128]{3,2,1,0:T(8,128)(2,1)S(1)}, bf16[4,2,128,128]{3,2,1,0:T(8,128)(2,1)S(1)}, u32[]{:S(2)}, u32[]{:S(2)}) collective-permute-start(bf16[4,2,128,128]{3,2,1,0:T(8,128)(2,1)S(1)} %get-tuple-element.71), channel_id=1, source_target_pairs={{0,240},{8,248},{16,0},{24,8},{32,16},{40,24},{48,32},{56,40},{64,... | collective-permute-start | bytes 786440 | tf_op jit(solution)/shard_map/ppermute | solution.py:375
  111.1 14.6 %collective-permute-start.13 = (bf16[4,2,128,128]{3,2,1,0:T(8,128)(2,1)S(1)}, bf16[4,2,128,128]{3,2,1,0:T(8,128)(2,1)S(1)}, u32[]{:S(2)}, u32[]{:S(2)}) collective-permute-start(bf16[4,2,128,128]{3,2,1,0:T(8,128)(2,1)S(1)} %get-tuple-element.70), channel_id=1, source_target_pairs={{0,248},{8,240},{16,8},{24,0},{32,24},{40,16},{48,40},{56,32},{64,... | collective-permute-start | bytes 786440 | tf_op jit(solution)/shard_map/ppermute | solution.py:375
  126.9 8.1 %collective-permute-start.14 = (bf16[2,128,128]{2,1,0:T(8,128)(2,1)S(1)}, bf16[2,128,128]{2,1,0:T(8,128)(2,1)S(1)}, u32[]{:S(2)}, u32[]{:S(2)}) collective-permute-start(bf16[2,128,128]{2,1,0:T(8,128)(2,1)S(1)} %get-tuple-element.78), channel_id=1, source_target_pairs={{0,6},{2,0},{4,2},{6,4},{1,7},{3,1},{5,3},{7,5},{8,14},{10,8},{12,... | collective-permute-start | bytes 196616 | tf_op jit(solution)/shard_map/ppermute | solution.py:362
  127.3 7.6 %collective-permute-start.15 = (bf16[2,128,128]{2,1,0:T(8,128)(2,1)S(1)}, bf16[2,128,128]{2,1,0:T(8,128)(2,1)S(1)}, u32[]{:S(2)}, u32[]{:S(2)}) collective-permute-start(bf16[2,128,128]{2,1,0:T(8,128)(2,1)S(1)} %get-tuple-element.80), channel_id=1, source_target_pairs={{0,4},{2,6},{4,0},{6,2},{1,5},{3,7},{5,1},{7,3},{8,12},{10,14},{12... | collective-permute-start | bytes 196616 | tf_op jit(solution)/shard_map/ppermute | solution.py:362
  129.9 5.1 %collective-permute-start.16 = (bf16[2,128,128]{2,1,0:T(8,128)(2,1)S(1)}, bf16[2,128,128]{2,1,0:T(8,128)(2,1)S(1)}, u32[]{:S(2)}, u32[]{:S(2)}) collective-permute-start(bf16[2,128,128]{2,1,0:T(8,128)(2,1)S(1)} %get-tuple-element.79), channel_id=1, source_target_pairs={{0,2},{2,4},{4,6},{6,0},{1,3},{3,5},{5,7},{7,1},{8,10},{10,12},{12... | collective-permute-start | bytes 196616 | tf_op jit(solution)/shard_map/ppermute | solution.py:362
